TPU v7x, 32 devices: a whole 2x2x4 slice. The times are simulated.
32 devices in a mesh: dp: 16 (over z, y, x), tensor: 2 (over core).
Axes of the slice: x: 2, y: 2, z: 4, core: 2. Of those that a mesh axis runs over, the one named last changes fastest.
Arguments:
- activations: bfloat16 [2560, 16384], P('dp', 'tensor'), may hold values from -6 to 6
- out_grads: bfloat16 [2560, 53248], P('dp', 'tensor'), may hold values from -6 to 6
- basis_in: bfloat16 [53248, 64], P('tensor'), may hold values from -6 to 6
Outputs:
- left_basis: float32 [16384, 64], P('tensor')
- basis_out: bfloat16 [53248, 64], P('tensor')
All inputs are finite; a program needn't handle non-finite values.
Results may differ from a plain program's by a relative error of at most 0.014.
Values may be sent and summed in bfloat16 or wider, within the bound.
A program may use at most 128 MiB of HBM per device.

v0:
```python
import jax
import jax.numpy as jnp
from jax import lax
from jax.sharding import PartitionSpec as P

D = 16384
FF = 53248


def factor_solve(block, gram, width):
    chol = jnp.linalg.cholesky(gram / width)
    return jax.scipy.linalg.solve_triangular(chol, block.T, lower=True).T


def local_gram(block):
    return jnp.dot(block.T, block, precision=lax.Precision.HIGHEST)


def per_device(activations, out_grads, basis_in):
    proj = lax.psum(
        jnp.dot(out_grads, basis_in, preferred_element_type=jnp.float32), "tensor"
    ).astype(jnp.bfloat16)
    left_part = lax.dot_general(
        activations, proj, (((0,), (0,)), ((), ())), preferred_element_type=jnp.float32
    )
    left = lax.psum(left_part, "dp")
    gram = lax.psum(local_gram(left), "tensor")
    left_basis = factor_solve(left, gram, D)
    back = lax.psum(
        jnp.dot(
            activations, left_basis.astype(jnp.bfloat16), preferred_element_type=jnp.float32
        ).astype(jnp.bfloat16),
        "tensor",
    )
    right_part = lax.dot_general(
        out_grads, back, (((0,), (0,)), ((), ())), preferred_element_type=jnp.float32
    )
    right = lax.psum(right_part, "dp")
    gram_right = lax.psum(local_gram(right), "tensor")
    basis_out = factor_solve(right, gram_right, FF).astype(jnp.bfloat16)
    return (left_basis, basis_out)


def solution(mesh):
    return jax.shard_map(
        per_device,
        mesh=mesh,
        in_specs=(P("dp", "tensor"), P("dp", "tensor"), P("tensor", None)),
        out_specs=(P("tensor", None), P("tensor", None)),
        check_vma=False,
    )
```

profile of v0, /device:TPU:0, one launch (start us, length us, event | category | flops | bytes accessed | tf_op | source)
XLA Modules:
  0.0 449.4 jit_solution(3060586462262724308)
XLA Ops:
  7.2 0.0 copy-start
  7.2 0.0 all-reduce.3.cloned.1.call-start
  7.2 1.9 copy-done
  9.1 5.8 %fusion.10 = f32[160,64]{1,0:T(8,128)S(1)} fusion(bf16[160,26624]{1,0:T(8,128)(2,1)} %param.5, bf16[26624,64]{0,1:T(8,128)(2,1)S(1)} %copy-done), kind=kOutput, calls=%fused_computation.26 | convolution fusion | flops 545259520 | bytes 11968512 | tf_op jit(solution)/shard_map/dot_general | solution.py:21
  14.9 3.9 psum.42
  18.8 3.7 convolution_bitcast_fusion.1
  22.5 0.0 all-reduce.3.cloned.1.call-update
  22.6 0.0 all-reduce.5.cloned.1.call-start
  22.6 128.5 %all-reduce.3.cloned.1.call-done = f32[8192,64]{0,1:T(8,128)} async-done(((f32[8192,64]{0,1:T(8,128)}), f32[8192,64]{0,1:T(8,128)}) %all-reduce.3.cloned.1.call-update) | async-done | bytes 2097168 | tf_op jit(solution)/shard_map/psum | solution.py:26
  151.1 4.0 fusion.11
  155.1 3.4 psum.44
  158.5 0.1 copy.6
  158.6 5.8 %cholesky.44 = f32[64,64]{1,0:T(8,128)S(1)} custom-call(f32[64,64]{1,0:T(8,128)S(1)} %fusion.9), custom_call_target="Cholesky" | custom-call | tf_op jit(solution)/shard_map/jit(cholesky)/cholesky | solution.py:11
  164.5 0.6 compare_reduce_fusion.1
  165.2 0.7 fusion.3
  165.8 4.9 %custom-call.10 = f32[1,64,64]{1,2,0:T(8,128)S(1)} custom-call(f32[1,64,64]{2,1,0:T(8,128)S(1)} %fusion.3), custom_call_target="InvertDiagBlocksLowerTriangular" | custom-call | tf_op jit(solution)/shard_map/jit(_solve_triangular)/triangular_solve | solution.py:12
  170.7 0.0 copy-start.1
  170.7 3.7 fusion.7
  174.4 0.0 copy-start.2
  174.4 1.3 copy-done.2
  175.7 0.0 copy-done.1
  175.7 1.0 fusion
  176.7 3.7 psum.45
  180.5 7.5 %convolution_bitcast_fusion = f32[26624,64]{0,1:T(8,128)} fusion(bf16[160,64]{0,1:T(8,128)(2,1)S(1)} %psum.45, bf16[160,26624]{1,0:T(8,128)(2,1)} %param.5), kind=kOutput, calls=%fused_computation | convolution fusion | flops 545259520 | bytes 15355904 | tf_op jit(solution)/shard_map/dot_general | solution.py:35
  188.0 0.0 all-reduce.5.cloned.1.call-update
  188.1 220.6 %all-reduce.5.cloned.1.call-done = f32[26624,64]{0,1:T(8,128)} async-done(((f32[26624,64]{0,1:T(8,128)}), f32[26624,64]{0,1:T(8,128)}) %all-reduce.5.cloned.1.call-update) | async-done | bytes 6815760 | tf_op jit(solution)/shard_map/psum | solution.py:38
  408.7 8.7 %fusion.12 = f32[64,64]{0,1:T(8,128)S(1)} fusion(f32[26624,64]{0,1:T(8,128)} %all-reduce.5.cloned.1.call-done), kind=kOutput, calls=%fused_computation.28 | convolution fusion | flops 1308622848 | bytes 6832128 | tf_op jit(solution)/shard_map/dot_general | solution.py:16
  417.4 3.4 psum.47
  420.9 0.1 copy.8
  421.0 5.8 %cholesky.55 = f32[64,64]{1,0:T(8,128)S(1)} custom-call(f32[64,64]{1,0:T(8,128)S(1)} %fusion.6), custom_call_target="Cholesky" | custom-call | tf_op jit(solution)/shard_map/jit(cholesky)/cholesky | solution.py:11
  426.9 0.6 compare_reduce_fusion
  427.5 0.7 fusion.4
  428.2 4.9 %custom-call.11 = f32[1,64,64]{1,2,0:T(8,128)S(1)} custom-call(f32[1,64,64]{2,1,0:T(8,128)S(1)} %fusion.4), custom_call_target="InvertDiagBlocksLowerTriangular" | custom-call | tf_op jit(solution)/shard_map/jit(_solve_triangular)/triangular_solve | solution.py:12
  433.1 9.5 %convolution_convert_fusion = bf16[26624,64]{0,1:T(8,128)(2,1)} fusion(f32[26624,64]{0,1:T(8,128)} %all-reduce.5.cloned.1.call-done, f32[1,64,64]{1,2,0:T(8,128)S(1)} %custom-call.11), kind=kOutput, calls=%fused_computation.1 | convolution fusion | flops 1310326784 | bytes 10240000 | tf_op jit(solution)/shard_map/jit(_solve_triangular)/triangular_solve | solution.py:12
  (6 shorter events, 0.1 us)
Async XLA Ops:
  7.2 2.0 copy-start
  7.2 143.9 %all-reduce.3.cloned.1.call-start = ((), (), s32[]{:S(2)}) async-start(), calls=%async_computation | async-start | bytes 4194304 | tf_op jit(solution)/shard_map/psum | solution.py:26
  22.6 386.2 %all-reduce.5.cloned.1.call-start = ((), (), s32[]{:S(2)}) async-start(), calls=%async_computation.1 | async-start | bytes 13631488 | tf_op jit(solution)/shard_map/psum | solution.py:38
  170.7 5.0 %copy-start.1 = (bf16[160,8192]{1,0:T(8,128)(2,1)S(1)}, bf16[160,8192]{1,0:T(8,128)(2,1)}, u32[]{:S(2)}) copy-start(bf16[160,8192]{1,0:T(8,128)(2,1)} %param.4) | copy-start | bytes 7864324
  174.4 1.3 copy-start.2
Sparse Core Ops, SparseCore 0:
  22.7 128.3 all-reduce.2
  188.2 220.4 all-reduce.4
where the time goes:
time: 450 us; the launch traced here: 449 us
  waiting for transfers between devices  349 us (78%)
  matrix products  43.9 us (10%)
  other arithmetic  24.2 us (5%)
  blocking collectives  14.5 us (3%)
  between operations  14.2 us (3%)
    psum x1, waiting for transfers between devices, per_device(): right = lax.psum(right_part, 'dp')  221 us
    psum x1, waiting for transfers between devices, per_device(): left = lax.psum(left_part, 'dp')  128 us
    another operation x2, matrix products, factor_solve(): return jax.scipy.linalg.solve_triangular(chol, block.T, lower=True).T  13.1 us
    another operation x6, other arithmetic, factor_solve(): chol = jnp.linalg.cholesky(gram / width)  13 us
    dot_general x2, matrix products, local_gram(): return jnp.dot(block.T, block, precision=lax.Precision.HIGHEST)  12.8 us
    another operation x4, other arithmetic, factor_solve(): return jax.scipy.linalg.solve_triangular(chol, block.T, lower=True).T  11.1 us
  transfers between devices with their start and end apart: 2, of which 2 were waited for; matrix products, arithmetic and copies ran while one was open for 0% of the time, Pallas kernels for 0%

commit v1 on v0

v1 whole, which is shorter than its diff:
```python
import functools

import jax
import jax.numpy as jnp
from jax import lax
from jax.experimental import pallas as pl
from jax.experimental.pallas import tpu as pltpu
from jax.sharding import PartitionSpec as P

LANES = 128
STREAMS = 3


def log2_of(n):
    k = n.bit_length() - 1
    return k if n == 1 << k else None


def plan_streams(width, n):
    k = log2_of(n)
    units = width // (n * LANES)
    streams, offset = [], 0
    for q in range(STREAMS):
        mine = units // STREAMS + (1 if q < units % STREAMS else 0)
        if mine == 0:
            continue
        bits = list(range(k - 1))
        turn = q % max(k - 1, 1)
        order = bits[turn:] + bits[:turn] + [k - 1]
        streams.append((offset, mine * n * LANES, order))
        offset += mine * n * LANES
    return streams


def cholqr_kernel(n, tensors, streams, width, part_ref, out_ref, *scratch):
    k, kt = log2_of(n), log2_of(tensors)
    stages = len(streams) * k
    recv = scratch[:stages]
    whole, gram_out, gram_in, elim = scratch[stages:stages + 4]
    rs_send, rs_recv, ag_send, ag_recv, g_send, g_recv = scratch[stages + 4:]
    rank = part_ref.shape[0]
    me = lax.axis_index("dp")
    core = lax.axis_index("tensor")

    def bit_of(b):
        return lax.rem(me // (1 << b), 2)

    def partner(b):
        return me + (1 << b) - 2 * (1 << b) * bit_of(b)

    def core_partner(b):
        bit = lax.rem(core // (1 << b), 2)
        return core + (1 << b) - 2 * (1 << b) * bit

    targets = [{"dp": partner(b)} for b in range(k)]
    targets += [{"tensor": core_partner(b)} for b in range(kt)]
    barrier = pltpu.get_barrier_semaphore()
    for target in targets:
        pl.semaphore_signal(barrier, inc=1, device_id=target, device_id_type=pl.DeviceIdType.MESH)
    pl.semaphore_wait(barrier, k + kt)

    def remote(src, dst, send, arrive, target):
        return pltpu.make_async_remote_copy(
            src_ref=src, dst_ref=dst, send_sem=send, recv_sem=arrive,
            device_id=target, device_id_type=pl.DeviceIdType.MESH,
        )

    def lanes(start, size):
        return pl.ds(pl.multiple_of(start, LANES), size)

    def rs_copy(q, s):
        offset, wide, order = streams[q]
        half = wide >> (s + 1)
        base = offset if s == 0 else 0
        src = part_ref if s == 0 else recv[q * k + s - 1]
        start = base + (1 - bit_of(order[s])) * half
        return remote(
            src.at[:, lanes(start, half)], recv[q * k + s],
            rs_send.at[q, s], rs_recv.at[q, s], targets[order[s]],
        )

    for q in range(len(streams)):
        rs_copy(q, 0).start()
    for s in range(k):
        for q, (offset, wide, order) in enumerate(streams):
            rs_copy(q, s).wait()
            half = wide >> (s + 1)
            tile = wide // n
            src = part_ref if s == 0 else recv[q * k + s - 1]
            start = (offset if s == 0 else 0) + bit_of(order[s]) * half
            here = recv[q * k + s]

            def add(i, _, src=src, here=here, start=start, tile=tile):
                to = lanes(i * tile, tile)
                mine = src[:, lanes(start + i * tile, tile)].astype(jnp.float32)
                here[:, to] = (mine + here[:, to].astype(jnp.float32)).astype(here.dtype)
                return 0

            lax.fori_loop(0, half // tile, add, 0)
            if s + 1 < k:
                rs_copy(q, s + 1).start()

    def place(q, s):
        offset, wide, order = streams[q]
        start = offset
        for j in range(s):
            start = start + bit_of(order[j]) * (wide >> (j + 1))
        return start

    def other(q, s):
        order = streams[q][2]
        half = streams[q][1] >> (s + 1)
        return place(q, s) + (1 - bit_of(order[s])) * half

    def ag_copy(q, s):
        offset, wide, order = streams[q]
        here = whole.at[:, lanes(place(q, s + 1), wide >> (s + 1))]
        return remote(here, here, ag_send.at[q, s], ag_recv.at[q, s], targets[order[s]])

    gram = jnp.zeros((rank, rank), jnp.float32)
    for q, (offset, wide, order) in enumerate(streams):
        chunk = recv[q * k + k - 1][...]
        whole[:, lanes(place(q, k), wide // n)] = chunk
        ag_copy(q, k - 1).start()
        gram = gram + lax.dot_general(
            chunk, chunk, (((1,), (1,)), ((), ())), preferred_element_type=jnp.float32
        )

    def ag_step(s):
        for q in range(len(streams)):
            ag_copy(q, s).wait()
            if s > 0:
                ag_copy(q, s - 1).start()

    for j in range(k + kt):
        target = targets[(j + k) % (k + kt)]
        gram_out[j] = gram
        copy = remote(gram_out.at[j], gram_in.at[j], g_send.at[j], g_recv.at[j], target)
        copy.start()
        copy.wait()
        gram = gram + gram_in[j]

    gram = gram / width
    row = lax.broadcasted_iota(jnp.int32, (rank, rank), 0)
    col = lax.broadcasted_iota(jnp.int32, (rank, rank), 1)
    elim[:, :rank] = gram
    elim[:, rank:] = jnp.where(row == col, 1.0, 0.0).astype(jnp.float32)
    wide_lane = lax.broadcasted_iota(jnp.int32, (rank, 2 * rank), 1)
    tall_row = lax.broadcasted_iota(jnp.int32, (rank, 1), 0)

    def eliminate(i, _):
        x = elim[...]
        pivot_row = elim[pl.ds(i, 1), :]
        column = jnp.sum(jnp.where(wide_lane == i, x, 0.0), axis=1, keepdims=True)
        pivot = jnp.sum(jnp.where(wide_lane[:1] == i, pivot_row, 0.0), axis=1, keepdims=True)
        factor = jnp.where(tall_row > i, column / pivot, 0.0)
        elim[...] = x - factor * pivot_row
        return 0

    cuts = [rank * j // (k - 1) for j in range(k)]
    for j in range(k - 1):
        ag_step(k - 1 - j)
        lax.fori_loop(cuts[j], cuts[j + 1], eliminate, 0)
    done = elim[...]
    diagonal = jnp.sum(jnp.where(row == col, done[:, :rank], 0.0), axis=1, keepdims=True)
    inverse = done[:, rank:] / jnp.sqrt(diagonal)
    high = inverse.astype(jnp.bfloat16)
    low = (inverse - high.astype(jnp.float32)).astype(jnp.bfloat16)

    def apply(start, size, tile):
        def step(i, _):
            at = lanes(start + i * tile, tile)
            rows = whole[:, at]
            out_ref[:, at] = (
                jnp.dot(high, rows, preferred_element_type=jnp.float32)
                + jnp.dot(low, rows, preferred_element_type=jnp.float32)
            ).astype(out_ref.dtype)
            return 0

        lax.fori_loop(0, size // tile, step, 0)

    for q, (offset, wide, order) in enumerate(streams):
        apply(place(q, 1), wide // 2, wide // n)
    ag_step(0)
    for q, (offset, wide, order) in enumerate(streams):
        apply(other(q, 0), wide // 2, wide // n)


def cholqr(part, n, tensors, width, dtype, collective_id):
    rank, local = part.shape
    k, kt = log2_of(n), log2_of(tensors)
    streams = plan_streams(local, n)
    recv = [
        pltpu.VMEM((rank, wide >> (s + 1)), jnp.bfloat16)
        for _, wide, _ in streams
        for s in range(k)
    ]
    dma = pltpu.SemaphoreType.DMA
    return pl.pallas_call(
        functools.partial(cholqr_kernel, n, tensors, streams, width),
        out_shape=jax.ShapeDtypeStruct((rank, local), dtype),
        in_specs=[pl.BlockSpec(memory_space=pltpu.VMEM)],
        out_specs=pl.BlockSpec(memory_space=pltpu.VMEM),
        scratch_shapes=recv + [
            pltpu.VMEM((rank, local), jnp.bfloat16),
            pltpu.VMEM((k + kt, rank, rank), jnp.float32),
            pltpu.VMEM((k + kt, rank, rank), jnp.float32),
            pltpu.VMEM((rank, 2 * rank), jnp.float32),
            dma((len(streams), k)), dma((len(streams), k)),
            dma((len(streams), k)), dma((len(streams), k)),
            dma((k + kt,)), dma((k + kt,)),
        ],
        compiler_params=pltpu.CompilerParams(
            collective_id=collective_id, has_side_effects=True,
            vmem_limit_bytes=32 * 1024 * 1024,
        ),
    )(part)


def plain_cholqr(part, width):
    total = lax.psum(part, "dp")
    gram = lax.psum(
        jnp.dot(total, total.T, precision=lax.Precision.HIGHEST), "tensor"
    )
    chol = jnp.linalg.cholesky(gram / width)
    return jax.scipy.linalg.solve_triangular(chol, total, lower=True)


def per_device(n, tensors, activations, out_grads, basis_in):
    def basis(part, dtype, collective_id):
        width = part.shape[1] * tensors
        k, kt = log2_of(n), log2_of(tensors)
        if k is None or k < 2 or kt is None or part.shape[1] % (n * LANES):
            return plain_cholqr(part, width).astype(dtype)
        return cholqr(part.astype(jnp.bfloat16), n, tensors, width, dtype, collective_id)

    proj = lax.psum(
        jnp.dot(out_grads, basis_in, preferred_element_type=jnp.float32), "tensor"
    ).astype(jnp.bfloat16)
    left_part = lax.dot_general(
        proj, activations, (((0,), (0,)), ((), ())), preferred_element_type=jnp.float32
    )
    left_basis = basis(left_part, jnp.float32, 0)
    back = lax.psum(
        lax.dot_general(
            activations, left_basis.astype(jnp.bfloat16), (((1,), (1,)), ((), ())),
            preferred_element_type=jnp.float32,
        ).astype(jnp.bfloat16),
        "tensor",
    )
    right_part = lax.dot_general(
        back, out_grads, (((0,), (0,)), ((), ())), preferred_element_type=jnp.float32
    )
    basis_out = basis(right_part, jnp.bfloat16, 1)
    return (left_basis.T, basis_out.T)


def solution(mesh):
    return jax.shard_map(
        functools.partial(per_device, mesh.shape["dp"], mesh.shape["tensor"]),
        mesh=mesh,
        in_specs=(P("dp", "tensor"), P("dp", "tensor"), P("tensor", None)),
        out_specs=(P("tensor", None), P("tensor", None)),
        check_vma=False,
    )
```

time: 450 us -> 171 us (0.38)
  waiting for transfers between devices: 349 us -> 0 us
  Pallas kernels: 0 us -> 142 us
  matrix products: 43.9 us -> 13.9 us
  other arithmetic: 24.2 us -> 0 us
  between operations: 14.2 us -> 0.73 us
  blocking collectives: 14.5 us -> 7.34 us
    psum x2 -> x0, waiting for transfers between devices: 349 us -> none  [the longest x1 221 us: per_device(): right = lax.psum(right_part, 'dp')]
    pallas_call x0 -> x2, Pallas kernels: none -> 142 us  [cholqr(): pl.pallas_call(functools.partial(cholqr_kernel, n, tensors, streams, widt...]
    another operation x10 -> x0, other arithmetic: 24.1 us -> none  [the longest x6 13 us: factor_solve(): chol = jnp.linalg.cholesky(gram / width)]
    dot_general x5 -> x3, matrix products: 25 us -> 8.19 us  [the longest x1 4.69 us: per_device(): lax.dot_general(back, out_grads, (((0,), (0,)), ((), ())), preferred_elem...]
    another operation x2 -> x0, matrix products: 13.1 us -> none  [factor_solve(): return jax.scipy.linalg.solve_triangular(chol, block.T, lower=True).T]
    psum x3 -> x1, blocking collectives: 10.6 us -> 3.41 us  [per_device(): lax.psum(lax.dot_general(activations, left_basis.astype(jnp.bfloat16), ((...]
  transfers between devices with their start and end apart: 2 -> 0, of which waited for: 2 -> 0; matrix products, arithmetic and copies ran while one was open for 0% -> 0% of each run, Pallas kernels for 0% -> 0%
where the time goes in v1:
time: 171 us
  Pallas kernels  142 us (83%)
  matrix products  13.9 us (8%)
  blocking collectives  7.34 us (4%)
  local copies, waits for them, and re-layouts  6.36 us (4%)
    pallas_call x2, Pallas kernels, cholqr(): pl.pallas_call(functools.partial(cholqr_kernel, n, tensors, streams, widt...  142 us
    unnamed x10, local copies, waits for them, and re-layouts  6.36 us
    dot_general x1, matrix products, per_device(): jnp.dot(out_grads, basis_in, preferred_element_type=jnp.float32)  5.75 us
    dot_general x1, matrix products, per_device(): lax.dot_general(back, out_grads, (((0,), (0,)), ((), ())), preferred_elem...  4.69 us
    psum x1, blocking collectives, per_device(): lax.psum(jnp.dot(out_grads, basis_in, preferred_element_type=jnp.float32)...  3.93 us

profile of v1, /device:TPU:0, one launch (start us, length us, event | category | flops | bytes accessed | tf_op | source)
XLA Modules:
  0.0 170.7 jit_solution(1076339219447738768)
XLA Ops:
  0.6 0.0 copy-start
  0.6 2.0 %copy-done = bf16[26624,64]{0,1:T(8,128)(2,1)S(1)} copy-done((bf16[26624,64]{0,1:T(8,128)(2,1)S(1)}, bf16[26624,64]{0,1:T(8,128)(2,1)}, u32[]{:S(2)}) %copy-start) | copy-done | bytes 3407896
  2.6 5.8 %fusion.3 = f32[160,64]{1,0:T(8,128)S(1)} fusion(bf16[160,26624]{1,0:T(8,128)(2,1)} %param.4, bf16[26624,64]{0,1:T(8,128)(2,1)S(1)} %copy-done), kind=kOutput, calls=%fused_computation.6 | convolution fusion | flops 545259520 | bytes 11968512 | tf_op jit(solution)/shard_map/dot_general | solution.py:238
  8.4 3.9 %psum.14 = bf16[160,64]{1,0:T(8,128)(2,1)S(1)} all-reduce(f32[160,64]{1,0:T(8,128)S(1)} %fusion.3), channel_id=1, replica_groups=mesh['dp'=16,'tensor'=2] {'tensor'}, use_global_device_ids=true, to_apply=%region_0.0 | all-reduce | flops 10240 | bytes 61440 | tf_op jit(solution)/shard_map/psum | solution.py:237
  12.3 0.0 copy-start.3
  12.3 2.5 %convolution_convert_fusion.1.part_ref = bf16[64,8192]{1,0:T(8,128)(2,1)S(1)} fusion(bf16[160,8192]{1,0:T(8,128)(2,1)} %param.3, bf16[160,64]{1,0:T(8,128)(2,1)S(1)} %psum.14), kind=kOutput, calls=%fused_computation.1 | convolution fusion | flops 168296448 | bytes 3690496 | tf_op jit(solution)/shard_map/dot_general | solution.py:240
  14.8 57.6 %shard_map.50 = f32[64,8192]{1,0:T(8,128)S(1)} custom-call(bf16[64,8192]{1,0:T(8,128)(2,1)S(1)} %convolution_convert_fusion.1.part_ref), custom_call_target="tpu_custom_call" | custom-call | tf_op jit(solution)/shard_map/pallas_call | solution.py:199
  72.4 0.0 copy-start.1
  72.4 1.3 copy-done.1
  73.8 0.0 copy-done.3
  73.8 1.0 fusion
  74.7 3.4 %psum.15 = bf16[160,64]{0,1:T(8,128)(2,1)S(1)} all-reduce(bf16[160,64]{0,1:T(8,128)(2,1)S(1)} %fusion), channel_id=1, replica_groups=mesh['dp'=16,'tensor'=2] {'tensor'}, use_global_device_ids=true, to_apply=%region_1.0 | all-reduce | flops 10240 | bytes 40960 | tf_op jit(solution)/shard_map/psum | solution.py:244
  78.2 4.7 %convolution_convert_fusion.part_ref = bf16[64,26624]{1,0:T(8,128)(2,1)S(1)} fusion(bf16[160,64]{0,1:T(8,128)(2,1)S(1)} %psum.15, bf16[160,26624]{1,0:T(8,128)(2,1)} %param.4), kind=kOutput, calls=%fused_computation | convolution fusion | flops 546963456 | bytes 11948032 | tf_op jit(solution)/shard_map/dot_general | solution.py:251
  82.9 0.0 copy-start.2
  82.9 84.7 %shard_map.51 = bf16[64,26624]{1,0:T(8,128)(2,1)S(1)} custom-call(bf16[64,26624]{1,0:T(8,128)(2,1)S(1)} %convolution_convert_fusion.part_ref), custom_call_target="tpu_custom_call" | custom-call | tf_op jit(solution)/shard_map/pallas_call | solution.py:199
  167.6 0.0 copy-done.2
  167.6 1.3 copy.7
  169.0 1.7 %copy.8 = bf16[26624,64]{0,1:T(8,128)(2,1)} copy(bf16[26624,64]{0,1:T(8,128)(2,1)S(1)} %bitcast.12) | data formatting | bytes 6815744
Async XLA Ops:
  0.6 2.0 %copy-start = (bf16[26624,64]{0,1:T(8,128)(2,1)S(1)}, bf16[26624,64]{0,1:T(8,128)(2,1)}, u32[]{:S(2)}) copy-start(bf16[26624,64]{0,1:T(8,128)(2,1)} %param.5) | copy-start | bytes 10223620
  12.3 61.5 %copy-start.3 = (bf16[160,8192]{1,0:T(8,128)(2,1)S(1)}, bf16[160,8192]{1,0:T(8,128)(2,1)}, u32[]{:S(2)}) copy-start(bf16[160,8192]{1,0:T(8,128)(2,1)} %param.3) | copy-start | bytes 7864324
  72.4 1.3 copy-start.1
  82.9 84.8 %copy-start.2 = (f32[64,8192]{1,0:T(8,128)S(1)}, f32[64,8192]{1,0:T(8,128)}, u32[]{:S(2)}) copy-start(f32[64,8192]{1,0:T(8,128)} %copy-done.1) | copy-start | bytes 6291460

commit v2 on v1

--- a/solution.py
+++ b/solution.py
@@ -8,7 +8,7 @@
 from jax.sharding import PartitionSpec as P
 
 LANES = 128
-STREAMS = 3
+STREAMS = 6
 
 
 def log2_of(n):
@@ -25,7 +25,7 @@
         if mine == 0:
             continue
         bits = list(range(k - 1))
-        turn = q % max(k - 1, 1)
+        turn = q % (k - 1)
         order = bits[turn:] + bits[:turn] + [k - 1]
         streams.append((offset, mine * n * LANES, order))
         offset += mine * n * LANES
@@ -83,7 +83,7 @@
         rs_copy(q, 0).start()
     for s in range(k):
         for q, (offset, wide, order) in enumerate(streams):
-            rs_copy(q, s).wait()
+            rs_copy(q, s).wait_recv()
             half = wide >> (s + 1)
             tile = wide // n
             src = part_ref if s == 0 else recv[q * k + s - 1]
@@ -128,17 +128,28 @@
 
     def ag_step(s):
         for q in range(len(streams)):
-            ag_copy(q, s).wait()
+            ag_copy(q, s).wait_recv()
             if s > 0:
                 ag_copy(q, s - 1).start()
 
+    def gram_copy(j):
+        return remote(
+            gram_out.at[j], gram_in.at[j], g_send.at[j], g_recv.at[j],
+            targets[(j + k) % (k + kt)],
+        )
+
+    gram_out[0] = gram
+    gram_copy(0).start()
+    gathered = k - 1
     for j in range(k + kt):
-        target = targets[(j + k) % (k + kt)]
-        gram_out[j] = gram
-        copy = remote(gram_out.at[j], gram_in.at[j], g_send.at[j], g_recv.at[j], target)
-        copy.start()
-        copy.wait()
+        gram_copy(j).wait_recv()
         gram = gram + gram_in[j]
+        if j + 1 < k + kt:
+            gram_out[j + 1] = gram
+            gram_copy(j + 1).start()
+        if j % 2 == 1 and gathered > 1:
+            ag_step(gathered)
+            gathered -= 1
 
     gram = gram / width
     row = lax.broadcasted_iota(jnp.int32, (rank, rank), 0)
@@ -157,33 +168,39 @@
         elim[...] = x - factor * pivot_row
         return 0
 
-    cuts = [rank * j // (k - 1) for j in range(k)]
-    for j in range(k - 1):
-        ag_step(k - 1 - j)
+    cuts = [rank * j // (gathered + 1) for j in range(gathered + 2)]
+    for j in range(gathered + 1):
         lax.fori_loop(cuts[j], cuts[j + 1], eliminate, 0)
+        if gathered - j > 0:
+            ag_step(gathered - j)
     done = elim[...]
     diagonal = jnp.sum(jnp.where(row == col, done[:, :rank], 0.0), axis=1, keepdims=True)
     inverse = done[:, rank:] / jnp.sqrt(diagonal)
     high = inverse.astype(jnp.bfloat16)
     low = (inverse - high.astype(jnp.float32)).astype(jnp.bfloat16)
-
-    def apply(start, size, tile):
+    both = jnp.concatenate([high, low], axis=0)
+    tile = n // 2 * LANES
+
+    def apply(start, size):
         def step(i, _):
             at = lanes(start + i * tile, tile)
-            rows = whole[:, at]
-            out_ref[:, at] = (
-                jnp.dot(high, rows, preferred_element_type=jnp.float32)
-                + jnp.dot(low, rows, preferred_element_type=jnp.float32)
-            ).astype(out_ref.dtype)
+            two = jnp.dot(both, whole[:, at], preferred_element_type=jnp.float32)
+            out_ref[:, at] = (two[:rank] + two[rank:]).astype(out_ref.dtype)
             return 0
 
         lax.fori_loop(0, size // tile, step, 0)
 
     for q, (offset, wide, order) in enumerate(streams):
-        apply(place(q, 1), wide // 2, wide // n)
+        apply(place(q, 1), wide // 2)
     ag_step(0)
     for q, (offset, wide, order) in enumerate(streams):
-        apply(other(q, 0), wide // 2, wide // n)
+        apply(other(q, 0), wide // 2)
+    for q in range(len(streams)):
+        for s in range(k):
+            rs_copy(q, s).wait_send()
+            ag_copy(q, s).wait_send()
+    for j in range(k + kt):
+        gram_copy(j).wait_send()
 
 
 def cholqr(part, n, tensors, width, dtype, collective_id):

time: 171 us -> 146 us (0.85)
  Pallas kernels: 142 us -> 117 us
    pallas_call x2, Pallas kernels: 142 us -> 117 us  [cholqr(): pl.pallas_call(functools.partial(cholqr_kernel, n, tensors, streams, widt...]
where the time goes in v2:
time: 146 us
  Pallas kernels  117 us (80%)
  matrix products  13.9 us (10%)
  blocking collectives  7.34 us (5%)
  local copies, waits for them, and re-layouts  6.36 us (4%)
    pallas_call x2, Pallas kernels, cholqr(): pl.pallas_call(functools.partial(cholqr_kernel, n, tensors, streams, widt...  117 us
    unnamed x10, local copies, waits for them, and re-layouts  6.36 us
    dot_general x1, matrix products, per_device(): jnp.dot(out_grads, basis_in, preferred_element_type=jnp.float32)  5.75 us
    dot_general x1, matrix products, per_device(): lax.dot_general(back, out_grads, (((0,), (0,)), ((), ())), preferred_elem...  4.69 us
    psum x1, blocking collectives, per_device(): lax.psum(jnp.dot(out_grads, basis_in, preferred_element_type=jnp.float32)...  3.93 us
    psum x1, blocking collectives, per_device(): lax.psum(lax.dot_general(activations, left_basis.astype(jnp.bfloat16), ((...  3.41 us

profile of v2, /device:TPU:0, one launch (start us, length us, event | category | flops | bytes accessed | tf_op | source)
XLA Modules:
  0.0 145.6 jit_solution(6116166418302023727)
XLA Ops:
  0.6 0.0 copy-start
  0.6 2.0 %copy-done = bf16[26624,64]{0,1:T(8,128)(2,1)S(1)} copy-done((bf16[26624,64]{0,1:T(8,128)(2,1)S(1)}, bf16[26624,64]{0,1:T(8,128)(2,1)}, u32[]{:S(2)}) %copy-start) | copy-done | bytes 3407896
  2.6 5.8 %fusion.3 = f32[160,64]{1,0:T(8,128)S(1)} fusion(bf16[160,26624]{1,0:T(8,128)(2,1)} %param.4, bf16[26624,64]{0,1:T(8,128)(2,1)S(1)} %copy-done), kind=kOutput, calls=%fused_computation.6 | convolution fusion | flops 545259520 | bytes 11968512 | tf_op jit(solution)/shard_map/dot_general | solution.py:255
  8.4 3.9 %psum.14 = bf16[160,64]{1,0:T(8,128)(2,1)S(1)} all-reduce(f32[160,64]{1,0:T(8,128)S(1)} %fusion.3), channel_id=1, replica_groups=mesh['dp'=16,'tensor'=2] {'tensor'}, use_global_device_ids=true, to_apply=%region_0.0 | all-reduce | flops 10240 | bytes 61440 | tf_op jit(solution)/shard_map/psum | solution.py:254
  12.3 0.0 copy-start.3
  12.3 2.5 %convolution_convert_fusion.1.part_ref = bf16[64,8192]{1,0:T(8,128)(2,1)S(1)} fusion(bf16[160,8192]{1,0:T(8,128)(2,1)} %param.3, bf16[160,64]{1,0:T(8,128)(2,1)S(1)} %psum.14), kind=kOutput, calls=%fused_computation.1 | convolution fusion | flops 168296448 | bytes 3690496 | tf_op jit(solution)/shard_map/dot_general | solution.py:257
  14.8 44.2 %shard_map.50 = f32[64,8192]{1,0:T(8,128)S(1)} custom-call(bf16[64,8192]{1,0:T(8,128)(2,1)S(1)} %convolution_convert_fusion.1.part_ref), custom_call_target="tpu_custom_call" | custom-call | tf_op jit(solution)/shard_map/pallas_call | solution.py:216
  59.0 0.0 copy-start.1
  59.0 1.3 copy-done.1
  60.3 0.0 copy-done.3
  60.3 1.0 fusion
  61.3 3.4 %psum.15 = bf16[160,64]{0,1:T(8,128)(2,1)S(1)} all-reduce(bf16[160,64]{0,1:T(8,128)(2,1)S(1)} %fusion), channel_id=1, replica_groups=mesh['dp'=16,'tensor'=2] {'tensor'}, use_global_device_ids=true, to_apply=%region_1.0 | all-reduce | flops 10240 | bytes 40960 | tf_op jit(solution)/shard_map/psum | solution.py:261
  64.7 4.7 %convolution_convert_fusion.part_ref = bf16[64,26624]{1,0:T(8,128)(2,1)S(1)} fusion(bf16[160,64]{0,1:T(8,128)(2,1)S(1)} %psum.15, bf16[160,26624]{1,0:T(8,128)(2,1)} %param.4), kind=kOutput, calls=%fused_computation | convolution fusion | flops 546963456 | bytes 11948032 | tf_op jit(solution)/shard_map/dot_general | solution.py:268
  69.4 0.0 copy-start.2
  69.5 73.1 %shard_map.51 = bf16[64,26624]{1,0:T(8,128)(2,1)S(1)} custom-call(bf16[64,26624]{1,0:T(8,128)(2,1)S(1)} %convolution_convert_fusion.part_ref), custom_call_target="tpu_custom_call" | custom-call | tf_op jit(solution)/shard_map/pallas_call | solution.py:216
  142.5 0.0 copy-done.2
  142.5 1.3 copy.7
  143.9 1.7 %copy.8 = bf16[26624,64]{0,1:T(8,128)(2,1)} copy(bf16[26624,64]{0,1:T(8,128)(2,1)S(1)} %bitcast.12) | data formatting | bytes 6815744
Async XLA Ops:
  0.6 2.0 %copy-start = (bf16[26624,64]{0,1:T(8,128)(2,1)S(1)}, bf16[26624,64]{0,1:T(8,128)(2,1)}, u32[]{:S(2)}) copy-start(bf16[26624,64]{0,1:T(8,128)(2,1)} %param.5) | copy-start | bytes 10223620
  12.3 48.0 %copy-start.3 = (bf16[160,8192]{1,0:T(8,128)(2,1)S(1)}, bf16[160,8192]{1,0:T(8,128)(2,1)}, u32[]{:S(2)}) copy-start(bf16[160,8192]{1,0:T(8,128)(2,1)} %param.3) | copy-start | bytes 7864324
  59.0 1.3 copy-start.1
  69.4 73.1 %copy-start.2 = (f32[64,8192]{1,0:T(8,128)S(1)}, f32[64,8192]{1,0:T(8,128)}, u32[]{:S(2)}) copy-start(f32[64,8192]{1,0:T(8,128)} %copy-done.1) | copy-start | bytes 6291460

commit v3 on v0

v3 whole, which is shorter than its diff:
```python
import functools

import jax
import jax.numpy as jnp
from jax import lax
from jax.experimental import pallas as pl
from jax.experimental.pallas import tpu as pltpu
from jax.sharding import PartitionSpec as P

LANES = 128
STREAMS = 6


def log2_of(n):
    k = n.bit_length() - 1
    return k if n == 1 << k else None


def plan_streams(width, n):
    k = log2_of(n)
    units = width // (n * LANES)
    streams, offset = [], 0
    for q in range(STREAMS):
        mine = units // STREAMS + (1 if q < units % STREAMS else 0)
        if mine == 0:
            continue
        bits = list(range(k - 1))
        turn = q % (k - 1)
        order = bits[turn:] + bits[:turn] + [k - 1]
        streams.append((offset, mine * n * LANES, order))
        offset += mine * n * LANES
    return streams


def power_kernel(
    n, tensors, sides, act_hbm, grad_hbm, left_part, left_out, right_out, *scratch
):
    k, kt = log2_of(n), log2_of(tensors)
    scratch = list(scratch)

    def take(count):
        taken = scratch[:count]
        del scratch[:count]
        return taken

    recvs = [take(len(streams) * k) for streams, _ in sides]
    left_whole, right_whole, right_part = take(3)
    gram_out, gram_in, elim, back_out, back_in, act, grad = take(7)
    side_sems = [take(6) for _ in sides]
    b_send, b_recv, load = take(3)
    rank = left_part.shape[0]
    me = lax.axis_index("dp")
    core = lax.axis_index("tensor")

    act_load = pltpu.make_async_copy(act_hbm, act, load.at[0])
    grad_load = pltpu.make_async_copy(grad_hbm, grad, load.at[1])
    act_load.start()
    grad_load.start()

    def bit_of(b):
        return lax.rem(me // (1 << b), 2)

    def partner(b):
        return me + (1 << b) - 2 * (1 << b) * bit_of(b)

    def core_partner(b):
        bit = lax.rem(core // (1 << b), 2)
        return core + (1 << b) - 2 * (1 << b) * bit

    targets = [{"dp": partner(b)} for b in range(k)]
    targets += [{"tensor": core_partner(b)} for b in range(kt)]
    barrier = pltpu.get_barrier_semaphore()
    for target in targets:
        pl.semaphore_signal(barrier, inc=1, device_id=target, device_id_type=pl.DeviceIdType.MESH)
    pl.semaphore_wait(barrier, k + kt)

    def remote(src, dst, send, arrive, target):
        return pltpu.make_async_remote_copy(
            src_ref=src, dst_ref=dst, send_sem=send, recv_sem=arrive,
            device_id=target, device_id_type=pl.DeviceIdType.MESH,
        )

    def lanes(start, size):
        return pl.ds(pl.multiple_of(start, LANES), size)

    tile = n // 2 * LANES

    def tiles(start, size, body):
        def step(i, _):
            body(lanes(start + i * tile, tile))
            return 0

        lax.fori_loop(0, size // tile, step, 0)

    row = lax.broadcasted_iota(jnp.int32, (rank, rank), 0)
    col = lax.broadcasted_iota(jnp.int32, (rank, rank), 1)
    wide_lane = lax.broadcasted_iota(jnp.int32, (rank, 2 * rank), 1)
    tall_row = lax.broadcasted_iota(jnp.int32, (rank, 1), 0)

    def eliminate(i, _):
        x = elim[...]
        pivot_row = elim[pl.ds(i, 1), :]
        column = jnp.sum(jnp.where(wide_lane == i, x, 0.0), axis=1, keepdims=True)
        pivot = jnp.sum(jnp.where(wide_lane[:1] == i, pivot_row, 0.0), axis=1, keepdims=True)
        factor = jnp.where(tall_row > i, column / pivot, 0.0)
        elim[...] = x - factor * pivot_row
        return 0

    def cholqr(side, part, whole, produce, beside, arrived):
        streams, width = sides[side]
        recv = recvs[side]
        rs_send, rs_recv, ag_send, ag_recv, g_send, g_recv = side_sems[side]
        count = len(streams)

        def rs_copy(q, s):
            offset, wide, order = streams[q]
            half = wide >> (s + 1)
            src = part if s == 0 else recv[q * k + s - 1]
            start = (offset if s == 0 else 0) + (1 - bit_of(order[s])) * half
            return remote(
                src.at[:, lanes(start, half)], recv[q * k + s],
                rs_send.at[q, s], rs_recv.at[q, s], targets[order[s]],
            )

        for q, (offset, wide, order) in enumerate(streams):
            produce(offset + (1 - bit_of(order[0])) * (wide // 2), wide // 2)
            rs_copy(q, 0).start()
        for q, (offset, wide, order) in enumerate(streams):
            produce(offset + bit_of(order[0]) * (wide // 2), wide // 2)
        beside()
        for s in range(k):
            for q, (offset, wide, order) in enumerate(streams):
                rs_copy(q, s).wait_recv()
                half = wide >> (s + 1)
                step = wide // n
                src = part if s == 0 else recv[q * k + s - 1]
                start = (offset if s == 0 else 0) + bit_of(order[s]) * half
                here = recv[q * k + s]

                def add(i, _, src=src, here=here, start=start, step=step):
                    to = lanes(i * step, step)
                    mine = src[:, lanes(start + i * step, step)].astype(jnp.float32)
                    here[:, to] = (mine + here[:, to].astype(jnp.float32)).astype(here.dtype)
                    return 0

                lax.fori_loop(0, half // step, add, 0)
                if s + 1 < k:
                    rs_copy(q, s + 1).start()

        def place(q, s):
            offset, wide, order = streams[q]
            start = offset
            for j in range(s):
                start = start + bit_of(order[j]) * (wide >> (j + 1))
            return start

        def ag_copy(q, s):
            offset, wide, order = streams[q]
            here = whole.at[:, lanes(place(q, s + 1), wide >> (s + 1))]
            return remote(here, here, ag_send.at[q, s], ag_recv.at[q, s], targets[order[s]])

        gram = jnp.zeros((rank, rank), jnp.float32)
        for q, (offset, wide, order) in enumerate(streams):
            chunk = recv[q * k + k - 1][...]
            whole[:, lanes(place(q, k), wide // n)] = chunk
            ag_copy(q, k - 1).start()
            gram = gram + lax.dot_general(
                chunk, chunk, (((1,), (1,)), ((), ())), preferred_element_type=jnp.float32
            )

        def ag_step(s):
            for q in range(count):
                ag_copy(q, s).wait_recv()
                if s > 0:
                    ag_copy(q, s - 1).start()

        def gram_copy(j):
            return remote(
                gram_out.at[side, j], gram_in.at[side, j], g_send.at[j], g_recv.at[j],
                targets[(j + k) % (k + kt)],
            )

        gram_out[side, 0] = gram
        gram_copy(0).start()
        gathered = k - 1
        for j in range(k + kt):
            gram_copy(j).wait_recv()
            gram = gram + gram_in[side, j]
            if j + 1 < k + kt:
                gram_out[side, j + 1] = gram
                gram_copy(j + 1).start()
            if j % 2 == 1 and gathered > 1:
                ag_step(gathered)
                gathered -= 1

        elim[:, :rank] = gram / width
        elim[:, rank:] = jnp.where(row == col, 1.0, 0.0).astype(jnp.float32)
        cuts = [rank * j // (gathered + 1) for j in range(gathered + 2)]
        for j in range(gathered + 1):
            lax.fori_loop(cuts[j], cuts[j + 1], eliminate, 0)
            if gathered - j > 0:
                ag_step(gathered - j)
        done = elim[...]
        diagonal = jnp.sum(jnp.where(row == col, done[:, :rank], 0.0), axis=1, keepdims=True)
        inverse = done[:, rank:] / jnp.sqrt(diagonal)
        finish = arrived(inverse)
        for q, (offset, wide, order) in enumerate(streams):
            finish(place(q, 1), wide // 2)
        ag_step(0)
        for q, (offset, wide, order) in enumerate(streams):
            finish(place(q, 0) + (1 - bit_of(order[0])) * (wide // 2), wide // 2)
        for q in range(count):
            for s in range(k):
                rs_copy(q, s).wait_send()
                ag_copy(q, s).wait_send()
        for j in range(k + kt):
            gram_copy(j).wait_send()
        return inverse

    def halves(inverse):
        high = inverse.astype(jnp.bfloat16)
        low = (inverse - high.astype(jnp.float32)).astype(jnp.bfloat16)
        return jnp.concatenate([high, low], axis=0)

    def apply(inverse, whole, out):
        both = halves(inverse)

        def body(at):
            two = jnp.dot(both, whole[:, at], preferred_element_type=jnp.float32)
            out[:, at] = (two[:rank] + two[rank:]).astype(out.dtype)

        return body

    back_out[0] = jnp.zeros_like(back_out[0])
    act_load.wait()

    def left_arrived(inverse):
        def body(at):
            back_out[0] += lax.dot_general(
                left_whole[:, at], act[:, at], (((1,), (1,)), ((), ())),
                preferred_element_type=jnp.float32,
            )

        return lambda start, size: tiles(start, size, body)

    left_inverse = cholqr(
        0, left_part, left_whole, lambda start, size: None, lambda: None, left_arrived
    )

    def back_copy(j):
        return remote(
            back_out.at[j], back_in.at[j], b_send.at[j], b_recv.at[j], targets[k + j]
        )

    total = back_out[0]
    for j in range(kt):
        if j > 0:
            back_out[j] = total
        back_copy(j).start()
        back_copy(j).wait()
        total = total + back_in[j]
    back = jnp.dot(
        left_inverse, total, precision=lax.Precision.HIGHEST,
        preferred_element_type=jnp.float32,
    ).astype(jnp.bfloat16)

    grad_load.wait()

    def multiply(at):
        right_part[:, at] = jnp.dot(
            back, grad[:, at], preferred_element_type=jnp.float32
        ).astype(right_part.dtype)

    def left_basis():
        tiles(0, left_out.shape[1], apply(left_inverse, left_whole, left_out))

    def right_arrived(inverse):
        body = apply(inverse, right_whole, right_out)
        return lambda start, size: tiles(start, size, body)

    cholqr(
        1, right_part, right_whole,
        lambda start, size: tiles(start, size, multiply), left_basis, right_arrived,
    )


def power_step(left_part, activations, out_grads, n, tensors):
    rank, left_local = left_part.shape
    tokens, right_local = out_grads.shape
    k, kt = log2_of(n), log2_of(tensors)
    locals_ = (left_local, right_local)
    sides = [(plan_streams(local, n), local * tensors) for local in locals_]
    recv = [
        pltpu.VMEM((rank, wide >> (s + 1)), jnp.bfloat16)
        for streams, _ in sides
        for _, wide, _ in streams
        for s in range(k)
    ]
    dma = pltpu.SemaphoreType.DMA
    sems = []
    for streams, _ in sides:
        sems += [dma((len(streams), k))] * 4 + [dma((k + kt,))] * 2
    back_slots = max(kt, 1)
    return pl.pallas_call(
        functools.partial(power_kernel, n, tensors, sides),
        out_shape=(
            jax.ShapeDtypeStruct((rank, left_local), jnp.float32),
            jax.ShapeDtypeStruct((rank, right_local), jnp.bfloat16),
        ),
        in_specs=[
            pl.BlockSpec(memory_space=pl.ANY),
            pl.BlockSpec(memory_space=pl.ANY),
            pl.BlockSpec(memory_space=pltpu.VMEM),
        ],
        out_specs=(
            pl.BlockSpec(memory_space=pltpu.VMEM),
            pl.BlockSpec(memory_space=pltpu.VMEM),
        ),
        scratch_shapes=recv + [
            pltpu.VMEM((rank, left_local), jnp.bfloat16),
            pltpu.VMEM((rank, right_local), jnp.bfloat16),
            pltpu.VMEM((rank, right_local), jnp.bfloat16),
            pltpu.VMEM((2, k + kt, rank, rank), jnp.float32),
            pltpu.VMEM((2, k + kt, rank, rank), jnp.float32),
            pltpu.VMEM((rank, 2 * rank), jnp.float32),
            pltpu.VMEM((back_slots, rank, tokens), jnp.float32),
            pltpu.VMEM((back_slots, rank, tokens), jnp.float32),
            pltpu.VMEM((tokens, left_local), jnp.bfloat16),
            pltpu.VMEM((tokens, right_local), jnp.bfloat16),
        ] + sems + [dma((back_slots,)), dma((back_slots,)), dma((2,))],
        compiler_params=pltpu.CompilerParams(
            collective_id=0, has_side_effects=True,
            vmem_limit_bytes=52 * 1024 * 1024,
        ),
    )(activations, out_grads, left_part)


def plain_cholqr(part, width):
    total = lax.psum(part, "dp")
    gram = lax.psum(
        jnp.dot(total, total.T, precision=lax.Precision.HIGHEST), "tensor"
    )
    chol = jnp.linalg.cholesky(gram / width)
    return jax.scipy.linalg.solve_triangular(chol, total, lower=True)


def plain_step(left_part, activations, out_grads, tensors):
    left_basis = plain_cholqr(left_part, activations.shape[1] * tensors)
    back = lax.psum(
        lax.dot_general(
            activations, left_basis.astype(jnp.bfloat16), (((1,), (1,)), ((), ())),
            preferred_element_type=jnp.float32,
        ).astype(jnp.bfloat16),
        "tensor",
    )
    right_part = lax.dot_general(
        back, out_grads, (((0,), (0,)), ((), ())), preferred_element_type=jnp.float32
    )
    right_basis = plain_cholqr(right_part, out_grads.shape[1] * tensors)
    return left_basis, right_basis.astype(jnp.bfloat16)


def per_device(n, tensors, activations, out_grads, basis_in):
    proj = lax.psum(
        jnp.dot(out_grads, basis_in, preferred_element_type=jnp.float32), "tensor"
    ).astype(jnp.bfloat16)
    left_part = lax.dot_general(
        proj, activations, (((0,), (0,)), ((), ())), preferred_element_type=jnp.float32
    )
    k, kt = log2_of(n), log2_of(tensors)
    aligned = all(x.shape[1] % (n * LANES) == 0 for x in (activations, out_grads))
    if k is None or k < 2 or kt is None or not aligned:
        left_basis, right_basis = plain_step(left_part, activations, out_grads, tensors)
    else:
        left_basis, right_basis = power_step(
            left_part.astype(jnp.bfloat16), activations, out_grads, n, tensors
        )
    return (left_basis.T, right_basis.T)


def solution(mesh):
    return jax.shard_map(
        functools.partial(per_device, mesh.shape["dp"], mesh.shape["tensor"]),
        mesh=mesh,
        in_specs=(P("dp", "tensor"), P("dp", "tensor"), P("tensor", None)),
        out_specs=(P("tensor", None), P("tensor", None)),
        check_vma=False,
    )
```

time: 450 us -> 143 us (0.32)
  waiting for transfers between devices: 349 us -> 0 us
  Pallas kernels: 0 us -> 122 us
  matrix products: 43.9 us -> 8.11 us
  other arithmetic: 24.2 us -> 0 us
  between operations: 14.2 us -> 0.68 us
  blocking collectives: 14.5 us -> 3.93 us
    psum x2 -> x0, waiting for transfers between devices: 349 us -> none  [the longest x1 221 us: per_device(): right = lax.psum(right_part, 'dp')]
    pallas_call x0 -> x1, Pallas kernels: none -> 122 us  [power_step(): pl.pallas_call(functools.partial(power_kernel, n, tensors, sides), out_sh...]
    another operation x10 -> x0, other arithmetic: 24.1 us -> none  [the longest x6 13 us: factor_solve(): chol = jnp.linalg.cholesky(gram / width)]
    dot_general x5 -> x1, matrix products: 25 us -> 2.36 us  [per_device(): lax.dot_general(proj, activations, (((0,), (0,)), ((), ())), preferred_el...]
    another operation x2 -> x0, matrix products: 13.1 us -> none  [factor_solve(): return jax.scipy.linalg.solve_triangular(chol, block.T, lower=True).T]
    psum x3 -> x0, blocking collectives: 10.6 us -> none  [the longest x1 3.75 us: per_device(): lax.psum(jnp.dot(activations, left_basis.astype(jnp.bfloat16), preferred_...]
  transfers between devices with their start and end apart: 2 -> 0, of which waited for: 2 -> 0; matrix products, arithmetic and copies ran while one was open for 0% -> 0% of each run, Pallas kernels for 0% -> 0%
where the time goes in v3:
time: 143 us; the launch traced here: 141 us
  Pallas kernels  122 us (85%)
  matrix products  8.11 us (6%)
  local copies, waits for them, and re-layouts  6.93 us (5%)
  blocking collectives  3.93 us (3%)
    pallas_call x1, Pallas kernels, power_step(): pl.pallas_call(functools.partial(power_kernel, n, tensors, sides), out_sh...  122 us
    unnamed x6, local copies, waits for them, and re-layouts  6.93 us
    dot_general x1, matrix products, per_device(): jnp.dot(out_grads, basis_in, preferred_element_type=jnp.float32)  5.75 us
    psum x1, blocking collectives, per_device(): lax.psum(jnp.dot(out_grads, basis_in, preferred_element_type=jnp.float32)...  3.93 us

profile of v3, /device:TPU:0, one launch (start us, length us, event | category | flops | bytes accessed | tf_op | source)
XLA Modules:
  0.0 141.4 jit_solution(16102533815031591177)
XLA Ops:
  0.6 0.0 copy-start
  0.6 2.0 %copy-done = bf16[26624,64]{0,1:T(8,128)(2,1)S(1)} copy-done((bf16[26624,64]{0,1:T(8,128)(2,1)S(1)}, bf16[26624,64]{0,1:T(8,128)(2,1)}, u32[]{:S(2)}) %copy-start) | copy-done | bytes 3407896
  2.6 5.8 %fusion.1 = f32[160,64]{1,0:T(8,128)S(1)} fusion(bf16[160,26624]{1,0:T(8,128)(2,1)} %grad_hbm.1, bf16[26624,64]{0,1:T(8,128)(2,1)S(1)} %copy-done), kind=kOutput, calls=%fused_computation.2 | convolution fusion | flops 545259520 | bytes 11968512 | tf_op jit(solution)/shard_map/dot_general | solution.py:365
  8.4 3.9 %psum.7 = bf16[160,64]{1,0:T(8,128)(2,1)S(1)} all-reduce(f32[160,64]{1,0:T(8,128)S(1)} %fusion.1), channel_id=1, replica_groups=mesh['dp'=16,'tensor'=2] {'tensor'}, use_global_device_ids=true, to_apply=%region_0.0 | all-reduce | flops 10240 | bytes 61440 | tf_op jit(solution)/shard_map/psum | solution.py:364
  12.3 2.4 %convolution_convert_fusion.left_part = bf16[64,8192]{1,0:T(8,128)(2,1)S(1)} fusion(bf16[160,8192]{1,0:T(8,128)(2,1)} %act_hbm.1, bf16[160,64]{1,0:T(8,128)(2,1)S(1)} %psum.7), kind=kOutput, calls=%fused_computation | convolution fusion | flops 168296448 | bytes 3690496 | tf_op jit(solution)/shard_map/dot_general | solution.py:367
  14.7 121.8 %shard_map.50 = (f32[64,8192]{1,0:T(8,128)}, bf16[64,26624]{1,0:T(8,128)(2,1)}) custom-call(bf16[160,8192]{1,0:T(8,128)(2,1)} %act_hbm.1, bf16[160,26624]{1,0:T(8,128)(2,1)} %grad_hbm.1, bf16[64,8192]{1,0:T(8,128)(2,1)S(1)} %convolution_convert_fusion.left_part), custom_call_target="tpu_custom_call" | custom-call | tf_op jit(solution)/shard_map/pallas_call | solution.py:304
  136.4 0.0 copy-start.1
  136.5 3.2 %copy.7 = f32[8192,64]{0,1:T(8,128)} copy(f32[8192,64]{0,1:T(8,128)} %bitcast.7) | data formatting | bytes 4194304
  139.7 0.0 copy-done.1
  139.7 1.8 %copy.8 = bf16[26624,64]{0,1:T(8,128)(2,1)} copy(bf16[26624,64]{0,1:T(8,128)(2,1)S(1)} %bitcast.6) | data formatting | bytes 6815744
Async XLA Ops:
  0.6 2.0 %copy-start = (bf16[26624,64]{0,1:T(8,128)(2,1)S(1)}, bf16[26624,64]{0,1:T(8,128)(2,1)}, u32[]{:S(2)}) copy-start(bf16[26624,64]{0,1:T(8,128)(2,1)} %param.5) | copy-start | bytes 10223620
  136.4 3.2 %copy-start.1 = (bf16[64,26624]{1,0:T(8,128)(2,1)S(1)}, bf16[64,26624]{1,0:T(8,128)(2,1)}, u32[]{:S(2)}) copy-start(bf16[64,26624]{1,0:T(8,128)(2,1)} %get-tuple-element.5) | copy-start | bytes 10223620

commit v4 on v3

--- a/solution.py
+++ b/solution.py
@@ -20,8 +20,11 @@
     k = log2_of(n)
     units = width // (n * LANES)
     streams, offset = [], 0
-    for q in range(STREAMS):
-        mine = units // STREAMS + (1 if q < units % STREAMS else 0)
+    shares = [units // STREAMS + (q < units % STREAMS) for q in range(STREAMS)]
+    if shares[-1] >= 2:
+        shares[-1] -= 1
+        shares[1] += 1
+    for q, mine in enumerate(shares):
         if mine == 0:
             continue
         bits = list(range(k - 1))
@@ -33,7 +36,7 @@
 
 
 def power_kernel(
-    n, tensors, sides, act_hbm, grad_hbm, left_part, left_out, right_out, *scratch
+    n, tensors, sides, act_hbm, grad_hbm, proj_part, left_out, right_out, *scratch
 ):
     k, kt = log2_of(n), log2_of(tensors)
     scratch = list(scratch)
@@ -44,11 +47,11 @@
         return taken
 
     recvs = [take(len(streams) * k) for streams, _ in sides]
-    left_whole, right_whole, right_part = take(3)
+    left_whole, left_part, right_whole, right_part = take(4)
     gram_out, gram_in, elim, back_out, back_in, act, grad = take(7)
     side_sems = [take(6) for _ in sides]
     b_send, b_recv, load = take(3)
-    rank = left_part.shape[0]
+    rank = proj_part.shape[0]
     me = lax.axis_index("dp")
     core = lax.axis_index("tensor")
 
@@ -231,12 +234,36 @@
 
         return body
 
-    back_out[0] = jnp.zeros_like(back_out[0])
+    def core_sum(use):
+        def copy(j):
+            return remote(
+                back_out.at[use, j], back_in.at[use, j],
+                b_send.at[use, j], b_recv.at[use, j], targets[k + j],
+            )
+
+        total = back_out[use, 0]
+        for j in range(kt):
+            if j > 0:
+                back_out[use, j] = total
+            copy(j).start()
+            copy(j).wait()
+            total = total + back_in[use, j]
+        return total
+
+    back_out[0, 0] = proj_part[...]
+    proj = core_sum(0).astype(jnp.bfloat16)
     act_load.wait()
+
+    def multiply_left(at):
+        left_part[:, at] = jnp.dot(
+            proj, act[:, at], preferred_element_type=jnp.float32
+        ).astype(left_part.dtype)
+
+    back_out[1, 0] = jnp.zeros_like(back_out[1, 0])
 
     def left_arrived(inverse):
         def body(at):
-            back_out[0] += lax.dot_general(
+            back_out[1, 0] += lax.dot_general(
                 left_whole[:, at], act[:, at], (((1,), (1,)), ((), ())),
                 preferred_element_type=jnp.float32,
             )
@@ -244,21 +271,11 @@
         return lambda start, size: tiles(start, size, body)
 
     left_inverse = cholqr(
-        0, left_part, left_whole, lambda start, size: None, lambda: None, left_arrived
-    )
-
-    def back_copy(j):
-        return remote(
-            back_out.at[j], back_in.at[j], b_send.at[j], b_recv.at[j], targets[k + j]
-        )
-
-    total = back_out[0]
-    for j in range(kt):
-        if j > 0:
-            back_out[j] = total
-        back_copy(j).start()
-        back_copy(j).wait()
-        total = total + back_in[j]
+        0, left_part, left_whole,
+        lambda start, size: tiles(start, size, multiply_left), lambda: None, left_arrived,
+    )
+
+    total = core_sum(1)
     back = jnp.dot(
         left_inverse, total, precision=lax.Precision.HIGHEST,
         preferred_element_type=jnp.float32,
@@ -284,8 +301,8 @@
     )
 
 
-def power_step(left_part, activations, out_grads, n, tensors):
-    rank, left_local = left_part.shape
+def power_step(proj_part, activations, out_grads, n, tensors):
+    rank, left_local = proj_part.shape[0], activations.shape[1]
     tokens, right_local = out_grads.shape
     k, kt = log2_of(n), log2_of(tensors)
     locals_ = (left_local, right_local)
@@ -304,7 +321,7 @@
     return pl.pallas_call(
         functools.partial(power_kernel, n, tensors, sides),
         out_shape=(
-            jax.ShapeDtypeStruct((rank, left_local), jnp.float32),
+            jax.ShapeDtypeStruct((rank, left_local), jnp.bfloat16),
             jax.ShapeDtypeStruct((rank, right_local), jnp.bfloat16),
         ),
         in_specs=[
@@ -318,21 +335,22 @@
         ),
         scratch_shapes=recv + [
             pltpu.VMEM((rank, left_local), jnp.bfloat16),
+            pltpu.VMEM((rank, left_local), jnp.bfloat16),
             pltpu.VMEM((rank, right_local), jnp.bfloat16),
             pltpu.VMEM((rank, right_local), jnp.bfloat16),
             pltpu.VMEM((2, k + kt, rank, rank), jnp.float32),
             pltpu.VMEM((2, k + kt, rank, rank), jnp.float32),
             pltpu.VMEM((rank, 2 * rank), jnp.float32),
-            pltpu.VMEM((back_slots, rank, tokens), jnp.float32),
-            pltpu.VMEM((back_slots, rank, tokens), jnp.float32),
+            pltpu.VMEM((2, back_slots, rank, tokens), jnp.float32),
+            pltpu.VMEM((2, back_slots, rank, tokens), jnp.float32),
             pltpu.VMEM((tokens, left_local), jnp.bfloat16),
             pltpu.VMEM((tokens, right_local), jnp.bfloat16),
-        ] + sems + [dma((back_slots,)), dma((back_slots,)), dma((2,))],
+        ] + sems + [dma((2, back_slots)), dma((2, back_slots)), dma((2,))],
         compiler_params=pltpu.CompilerParams(
             collective_id=0, has_side_effects=True,
             vmem_limit_bytes=52 * 1024 * 1024,
         ),
-    )(activations, out_grads, left_part)
+    )(activations, out_grads, proj_part)
 
 
 def plain_cholqr(part, width):
@@ -344,7 +362,9 @@
     return jax.scipy.linalg.solve_triangular(chol, total, lower=True)
 
 
-def plain_step(left_part, activations, out_grads, tensors):
+def plain_step(proj_part, activations, out_grads, tensors):
+    proj = lax.psum(proj_part, "tensor").astype(jnp.bfloat16)
+    left_part = jnp.dot(proj, activations, preferred_element_type=jnp.float32)
     left_basis = plain_cholqr(left_part, activations.shape[1] * tensors)
     back = lax.psum(
         lax.dot_general(
@@ -361,20 +381,18 @@
 
 
 def per_device(n, tensors, activations, out_grads, basis_in):
-    proj = lax.psum(
-        jnp.dot(out_grads, basis_in, preferred_element_type=jnp.float32), "tensor"
-    ).astype(jnp.bfloat16)
-    left_part = lax.dot_general(
-        proj, activations, (((0,), (0,)), ((), ())), preferred_element_type=jnp.float32
+    proj_part = lax.dot_general(
+        basis_in, out_grads, (((0,), (1,)), ((), ())), preferred_element_type=jnp.float32
     )
     k, kt = log2_of(n), log2_of(tensors)
     aligned = all(x.shape[1] % (n * LANES) == 0 for x in (activations, out_grads))
     if k is None or k < 2 or kt is None or not aligned:
-        left_basis, right_basis = plain_step(left_part, activations, out_grads, tensors)
+        left_basis, right_basis = plain_step(proj_part, activations, out_grads, tensors)
     else:
         left_basis, right_basis = power_step(
-            left_part.astype(jnp.bfloat16), activations, out_grads, n, tensors
+            proj_part, activations, out_grads, n, tensors
         )
+        left_basis = left_basis.astype(jnp.float32)
     return (left_basis.T, right_basis.T)
 
 

time: 143 us -> 141 us (0.986); the launches traced: 141 us -> 141 us
  Pallas kernels: 122 us -> 127 us
  blocking collectives: 3.93 us -> 0 us
  matrix products: 8.11 us -> 6.34 us
  other arithmetic: 0 us -> 1.46 us
    pallas_call x1, Pallas kernels: 122 us -> 127 us  [power_step(): pl.pallas_call(functools.partial(power_kernel, n, tensors, sides), out_sh...]
    psum x1 -> x0, blocking collectives: 3.93 us -> none  [per_device(): lax.psum(jnp.dot(out_grads, basis_in, preferred_element_type=jnp.float32)...]
    dot_general x2 -> x1, matrix products: 8.11 us -> 6.34 us  [per_device(): lax.dot_general(basis_in, out_grads, (((0,), (1,)), ((), ())), preferred_...]
    transpose x0 -> x1, other arithmetic: none -> 1.46 us  [per_device(): return (left_basis.T, right_basis.T)]
    unnamed x6 -> x3, local copies, waits for them, and re-layouts: 6.93 us -> 5.89 us
where the time goes in v4:
time: 141 us
  Pallas kernels  127 us (90%)
  matrix products  6.34 us (4%)
  local copies, waits for them, and re-layouts  5.89 us (4%)
  other arithmetic  1.46 us (1%)
    pallas_call x1, Pallas kernels, power_step(): pl.pallas_call(functools.partial(power_kernel, n, tensors, sides), out_sh...  127 us
    dot_general x1, matrix products, per_device(): lax.dot_general(basis_in, out_grads, (((0,), (1,)), ((), ())), preferred_...  6.34 us
    unnamed x3, local copies, waits for them, and re-layouts  5.89 us

profile of v4, /device:TPU:0, one launch (start us, length us, event | category | flops | bytes accessed | tf_op | source)
XLA Modules:
  0.0 141.3 jit_solution(4128346268553816659)
XLA Ops:
  0.6 0.0 copy-start
  0.6 2.0 %copy-done = bf16[26624,64]{0,1:T(8,128)(2,1)S(1)} copy-done((bf16[26624,64]{0,1:T(8,128)(2,1)S(1)}, bf16[26624,64]{0,1:T(8,128)(2,1)}, u32[]{:S(2)}) %copy-start) | copy-done | bytes 3407896
  2.6 6.3 %fusion.proj_part = f32[64,160]{1,0:T(8,128)S(1)} fusion(bf16[26624,64]{0,1:T(8,128)(2,1)S(1)} %copy-done, bf16[160,26624]{1,0:T(8,128)(2,1)} %grad_hbm.1), kind=kOutput, calls=%fused_computation.1 | convolution fusion | flops 545259520 | bytes 11968512 | tf_op jit(solution)/shard_map/dot_general | solution.py:384
  8.9 126.9 %shard_map.50 = (bf16[64,8192]{1,0:T(8,128)(2,1)S(1)}, bf16[64,26624]{1,0:T(8,128)(2,1)}) custom-call(bf16[160,8192]{1,0:T(8,128)(2,1)} %act_hbm.1, bf16[160,26624]{1,0:T(8,128)(2,1)} %grad_hbm.1, f32[64,160]{1,0:T(8,128)S(1)} %fusion.proj_part), custom_call_target="tpu_custom_call" | custom-call | tf_op jit(solution)/shard_map/pallas_call | solution.py:321
  135.9 1.5 %convert_bitcast_fusion = f32[8192,64]{0,1:T(8,128)} fusion(bf16[64,8192]{1,0:T(8,128)(2,1)S(1)} %get-tuple-element.4), kind=kLoop, calls=%fused_computation | loop fusion | flops 524288 | bytes 3145728 | tf_op jit(solution)/shard_map/transpose | solution.py:396
  137.3 3.9 %copy.6 = bf16[26624,64]{0,1:T(8,128)(2,1)} copy(bf16[26624,64]{0,1:T(8,128)(2,1)} %bitcast.5) | data formatting | bytes 6815744
Async XLA Ops:
  0.6 2.0 %copy-start = (bf16[26624,64]{0,1:T(8,128)(2,1)S(1)}, bf16[26624,64]{0,1:T(8,128)(2,1)}, u32[]{:S(2)}) copy-start(bf16[26624,64]{0,1:T(8,128)(2,1)} %param.5) | copy-start | bytes 10223620

commit v5 on v4

--- a/solution.py
+++ b/solution.py
@@ -348,7 +348,7 @@
         ] + sems + [dma((2, back_slots)), dma((2, back_slots)), dma((2,))],
         compiler_params=pltpu.CompilerParams(
             collective_id=0, has_side_effects=True,
-            vmem_limit_bytes=52 * 1024 * 1024,
+            vmem_limit_bytes=36 * 1024 * 1024,
         ),
     )(activations, out_grads, proj_part)
 

time: 141 us -> 139 us (0.986)
  local copies, waits for them, and re-layouts: 5.89 us -> 3.71 us
    unnamed x3 -> x7, local copies, waits for them, and re-layouts: 5.89 us -> 3.71 us
where the time goes in v5:
time: 139 us
  Pallas kernels  126 us (91%)
  matrix products  7.11 us (5%)
  local copies, waits for them, and re-layouts  3.71 us (3%)
  other arithmetic  1.46 us (1%)
    pallas_call x1, Pallas kernels, power_step(): pl.pallas_call(functools.partial(power_kernel, n, tensors, sides), out_sh...  126 us
    dot_general x1, matrix products, per_device(): lax.dot_general(basis_in, out_grads, (((0,), (1,)), ((), ())), preferred_...  7.11 us
    unnamed x7, local copies, waits for them, and re-layouts  3.71 us

profile of v5, /device:TPU:0, one launch (start us, length us, event | category | flops | bytes accessed | tf_op | source)
XLA Modules:
  0.0 139.1 jit_solution(3903466238640895916)
XLA Ops:
  0.6 0.0 copy-start
  0.6 0.0 copy-start.1
  0.7 1.9 %copy-done = bf16[26624,64]{0,1:T(8,128)(2,1)S(1)} copy-done((bf16[26624,64]{0,1:T(8,128)(2,1)S(1)}, bf16[26624,64]{0,1:T(8,128)(2,1)}, u32[]{:S(2)}) %copy-start) | copy-done | bytes 3407896
  2.6 0.0 copy-start.2
  2.6 7.1 %fusion.proj_part = f32[64,160]{1,0:T(8,128)S(1)} fusion(bf16[26624,64]{0,1:T(8,128)(2,1)S(1)} %copy-done, bf16[160,26624]{1,0:T(8,128)(2,1)} %grad_hbm.1), kind=kOutput, calls=%fused_computation.1 | convolution fusion | flops 545259520 | bytes 11968512 | tf_op jit(solution)/shard_map/dot_general | solution.py:384
  9.7 0.0 copy-done.1
  9.7 0.0 copy-done.2
  9.7 126.1 %shard_map.50 = (bf16[64,8192]{1,0:T(8,128)(2,1)S(1)}, bf16[64,26624]{1,0:T(8,128)(2,1)S(1)}) custom-call(bf16[160,8192]{1,0:T(8,128)(2,1)S(1)} %copy-done.2, bf16[160,26624]{1,0:T(8,128)(2,1)S(1)} %copy-done.1, f32[64,160]{1,0:T(8,128)S(1)} %fusion.proj_part), custom_call_target="tpu_custom_call" | custom-call | tf_op jit(solution)/shard_map/pallas_call | solution.py:321
  135.9 1.5 %convert_bitcast_fusion = f32[8192,64]{0,1:T(8,128)} fusion(bf16[64,8192]{1,0:T(8,128)(2,1)S(1)} %get-tuple-element.4), kind=kLoop, calls=%fused_computation | loop fusion | flops 524288 | bytes 3145728 | tf_op jit(solution)/shard_map/transpose | solution.py:396
  137.3 1.7 %copy.6 = bf16[26624,64]{0,1:T(8,128)(2,1)} copy(bf16[26624,64]{0,1:T(8,128)(2,1)S(1)} %bitcast.5) | data formatting | bytes 6815744
Async XLA Ops:
  0.6 2.0 %copy-start = (bf16[26624,64]{0,1:T(8,128)(2,1)S(1)}, bf16[26624,64]{0,1:T(8,128)(2,1)}, u32[]{:S(2)}) copy-start(bf16[26624,64]{0,1:T(8,128)(2,1)} %param.5) | copy-start | bytes 10223620
  0.6 9.1 %copy-start.1 = (bf16[160,26624]{1,0:T(8,128)(2,1)S(1)}, bf16[160,26624]{1,0:T(8,128)(2,1)}, u32[]{:S(2)}) copy-start(bf16[160,26624]{1,0:T(8,128)(2,1)} %grad_hbm.1) | copy-start | bytes 25559044
  2.6 7.1 %copy-start.2 = (bf16[160,8192]{1,0:T(8,128)(2,1)S(1)}, bf16[160,8192]{1,0:T(8,128)(2,1)}, u32[]{:S(2)}) copy-start(bf16[160,8192]{1,0:T(8,128)(2,1)} %act_hbm.1) | copy-start | bytes 7864324
